TPU v7x, 32 devices: a whole 2x2x4 slice. The times are simulated.
32 devices in a mesh: ep: 8 (over z, x), node: 2 (over core), dp: 2 (over y).
Axes of the slice: x: 2, y: 2, z: 4, core: 2. Of those that a mesh axis runs over, the one named last changes fastest.
Arguments:
- grad_out: bfloat16 [2048, 7168], P(('ep', 'node'), 'dp'), may hold values from -6 to 6
- tokens: bfloat16 [2048, 7168], P(('ep', 'node'), 'dp'), may hold values from -0.59765625 to 0.59765625
- scores: float32 [2048, 16], P(('ep', 'node')), may hold values from 0.02 to 0.98
- expert_ids: int32 [2048, 8], P(('ep', 'node')), may hold values from 0 to 15, all different within a row; in each aligned block of 128 rows (0 to 127, 128 to 255, ...) at most 80 rows name the same one
- hidden_act: bfloat16 [16, 1280, 1024], P(('ep', 'node')), may hold values from -0.29882812 to 0.29882812
- down_weight: bfloat16 [16, 1024, 7168], P(('ep', 'node'), None, 'dp'), may hold values from -0.1875 to 0.1875
Outputs:
- weight_grad: bfloat16 [16, 1024, 7168], P(('ep', 'node'), None, 'dp')
- hidden_grad: bfloat16 [16, 1280, 1024], P(('ep', 'node'), 'dp')
- gate_grad: float32 [16, 7168], P(None, 'dp')
Inputs may be any that keep to these rules, and one draw needn't show every extreme that they name: `expert_ids`: among the routes of the 128 tokens of one source device, no expert is named more than 80 times, a bound that some block reaches.
All inputs are finite; a program needn't handle non-finite values.
Results may differ from a plain program's by a relative error of at most 0.017.
Values may be sent and summed in bfloat16 or wider, within the bound.
A program may use at most 128 MiB of HBM per device.

v0:
```python
import jax
import jax.numpy as jnp
from jax import lax
from jax.experimental import pallas as pl
from jax.experimental.pallas import tpu as pltpu
from jax.sharding import PartitionSpec as P
import functools

route_scale = 2.5
AX = ("ep", "node")
f32, bf16 = jnp.float32, jnp.bfloat16


def router(scores, expert_ids):
    tok = expert_ids.shape[0]
    experts = scores.shape[1]
    ids_t = expert_ids.T
    names = lax.broadcasted_iota(jnp.int32, (experts, tok), 0)
    mask = jnp.zeros((experts, tok), f32)
    for k in range(expert_ids.shape[1]):
        mask = mask + (ids_t[k][None, :] == names).astype(f32)
    chosen = mask * scores.T
    total = jnp.sum(chosen, axis=0, keepdims=True)
    gains = (route_scale * chosen / total).astype(bf16)
    before = (
        lax.broadcasted_iota(jnp.int32, (tok, tok), 0)
        < lax.broadcasted_iota(jnp.int32, (tok, tok), 1)
    ).astype(bf16)
    rank = jnp.dot(mask.astype(bf16), before, preferred_element_type=f32)
    rank = jnp.where(mask > 0, rank, -4096.0)
    return mask, chosen, total, gains, rank


MESH = pl.DeviceIdType.MESH
VM = pl.BlockSpec(memory_space=pltpu.VMEM)
ANY = pl.BlockSpec(memory_space=pl.ANY)


def gather_kernel(ep_n, inner, node_n, block, place, every, meta, local_sem,
                  send, recv, meta_send, meta_recv):
    outer = ep_n // inner
    ep, node = lax.axis_index("ep"), lax.axis_index("node")
    z, x = ep // inner, ep % inner
    n = ep_n * node_n
    me = ep * node_n + node

    def dev(zz, xx, cc):
        return {"ep": zz * inner + xx, "node": cc}

    def source(zz, xx, cc):
        return (zz * inner + xx) * node_n + cc

    barrier = pltpu.get_barrier_semaphore()

    def greet(j, carry):
        p = lax.rem(me + j, n)
        pl.semaphore_signal(barrier, inc=1, device_id={"ep": p // node_n, "node": p % node_n},
                            device_id_type=MESH)
        return carry

    lax.fori_loop(1, n, greet, 0)
    pl.semaphore_wait(barrier, n - 1)

    def push(way, s, to, own=False):
        pltpu.make_async_remote_copy(
            src_ref=block if own else every.at[s], dst_ref=every.at[s],
            send_sem=send.at[way, s], recv_sem=recv.at[s],
            device_id=to, device_id_type=MESH).start()

    def sent(way, s):
        pltpu.make_async_remote_copy(
            src_ref=every.at[s], dst_ref=every.at[s],
            send_sem=send.at[way, s], recv_sem=recv.at[s],
            device_id=dev(z, x, node), device_id_type=MESH).wait_send()

    def arrived(s):
        pltpu.make_async_remote_copy(
            src_ref=every.at[s], dst_ref=every.at[s],
            send_sem=send.at[0, s], recv_sem=recv.at[s],
            device_id=dev(z, x, node), device_id_type=MESH).wait_recv()

    def when(*conds):
        c = conds[0]
        for d in conds[1:]:
            c = jnp.logical_and(c, d)
        return pl.when(c)

    def start_x(s, up, down, own=False):
        @pl.when(up)
        def _():
            push(2, s, dev(z, x + 1, node), own)

        @pl.when(down)
        def _():
            push(3, s, dev(z, x - 1, node), own)

    def start_core(s, own=False):
        for k in range(1, node_n):
            push(3 + k, s, dev(z, x, lax.rem(node + k, node_n)), own)

    can_zu, can_zd = z + 1 < outer, z >= 1
    can_xu, can_xd = x + 1 < inner, x >= 1

    @pl.when(can_zu)
    def _():
        push(0, me, dev(z + 1, x, node), True)

    @pl.when(can_zd)
    def _():
        push(1, me, dev(z - 1, x, node), True)

    start_x(me, can_xu, can_xd, True)

    def tell(j, carry):
        p = lax.rem(me + j, n)
        pltpu.make_async_remote_copy(
            src_ref=place.at[p], dst_ref=meta.at[me],
            send_sem=meta_send.at[j], recv_sem=meta_recv.at[j],
            device_id={"ep": p // node_n, "node": p % node_n}, device_id_type=MESH).start()
        return carry

    lax.fori_loop(1, n, tell, 0)
    start_core(me, True)
    keep = pltpu.make_async_copy(block, every.at[me], local_sem)
    keep.start()
    meta[me] = place[me]

    def z_rows(t):
        if t == 0:
            return [(z >= 0, z, None)]
        return [(z >= t, z - t, True), (z + t < outer, z + t, False)]

    def x_step(t):
        for exists, row, _ in z_rows(t):
            for d in range(1, inner):
                s_low = source(row, x - d, node)
                s_high = source(row, x + d, node)

                @when(exists, x >= d)
                def _():
                    arrived(s_low)
                    start_core(s_low)

                    @pl.when(can_xu)
                    def _():
                        push(2, s_low, dev(z, x + 1, node))

                @when(exists, x + d < inner)
                def _():
                    arrived(s_high)
                    start_core(s_high)

                    @pl.when(can_xd)
                    def _():
                        push(3, s_high, dev(z, x - 1, node))

    for t in range(1, outer):
        for exists, row, below in z_rows(t):
            s = source(row, x, node)

            @pl.when(exists)
            def _():
                arrived(s)
                if below:
                    @pl.when(can_zu)
                    def _():
                        push(0, s, dev(z + 1, x, node))
                else:
                    @pl.when(can_zd)
                    def _():
                        push(1, s, dev(z - 1, x, node))
                start_x(s, can_xu, can_xd)
                start_core(s)
        x_step(t - 1)
    x_step(outer - 1)

    keep.wait()

    def rest(e, carry):
        for k in range(1, node_n):
            arrived(e * node_n + lax.rem(node + k, node_n))
        return carry

    lax.fori_loop(0, ep_n, rest, 0)

    def ended(e, carry):
        s = e * node_n + node
        row, col = e // inner, e % inner
        mine = col == x

        @when(mine, row <= z, can_zu)
        def _():
            sent(0, s)

        @when(mine, row >= z, can_zd)
        def _():
            sent(1, s)

        @when(col <= x, can_xu)
        def _():
            sent(2, s)

        @when(col >= x, can_xd)
        def _():
            sent(3, s)

        for k in range(1, node_n):
            sent(3 + k, s)
        return carry

    lax.fori_loop(0, ep_n, ended, 0)

    def told(j, carry):
        pltpu.make_async_remote_copy(
            src_ref=place.at[0], dst_ref=meta.at[0],
            send_sem=meta_send.at[j], recv_sem=meta_recv.at[j],
            device_id=dev(z, x, node), device_id_type=MESH).wait()
        return carry

    lax.fori_loop(1, n, told, 0)


def gather(ep_n, inner, node_n, grad_out, place):
    n = ep_n * node_n
    return pl.pallas_call(
        functools.partial(gather_kernel, ep_n, inner, node_n),
        out_shape=(jax.ShapeDtypeStruct((n,) + grad_out.shape, grad_out.dtype),
                   jax.ShapeDtypeStruct(place.shape, place.dtype)),
        in_specs=[ANY, VM],
        out_specs=(ANY, VM),
        scratch_shapes=[
            pltpu.SemaphoreType.DMA,
            pltpu.SemaphoreType.DMA((3 + node_n, n)),
            pltpu.SemaphoreType.DMA((n,)),
            pltpu.SemaphoreType.DMA((n,)),
            pltpu.SemaphoreType.DMA((n,)),
        ],
        compiler_params=pltpu.CompilerParams(collective_id=0, has_side_effects=True,
                                             vmem_limit_bytes=16 << 20),
        name="gather",
    )(grad_out, place)


def through_kernel(group, most, tok, every, meta, down, hidden, scaled, partial, back, pick, gain, total, plain):
    step, steps = pl.program_id(0), pl.num_programs(0)
    n = every.shape[0]
    rows = group * most

    def hits(g):
        for j in range(group):
            ranks = meta[g * group + j, 0:1, :]
            local = lax.broadcasted_iota(jnp.int32, (rows, tok), 0).astype(f32) - float(j * most)
            yield j, (ranks == local)

    @pl.when(step == 0)
    def _():
        total[...] = jnp.zeros_like(total)
        for g in range(n // group):
            own = jnp.zeros((rows, 1), f32)
            for j, hit in hits(g):
                own = own + jnp.sum(jnp.where(hit, meta[g * group + j, 1:2, :], 0.0), axis=1, keepdims=True)
                pick[g * group + j] = hit.astype(f32).astype(bf16)
            gain[g * rows:(g + 1) * rows, :] = own

    for g in range(n // group):
        got = jnp.zeros((rows, every.shape[2]), f32)
        for j in range(group):
            got = got + jnp.dot(pick[g * group + j], every[g * group + j], preferred_element_type=f32)
        span = slice(g * rows, (g + 1) * rows)
        scaled[span, :] = (got * gain[span, :]).astype(bf16)
        plain[span, :] = got.astype(bf16)
    total[...] += lax.dot_general(plain[...], down[...], (((1,), (1,)), ((), ())), preferred_element_type=f32)

    @pl.when(step == steps - 1)
    def _():
        for g in range(n // group):
            span = slice(g * rows, (g + 1) * rows)
            u = total[span, :]
            partial[span, :] = (gain[span, :] * u).astype(bf16)
            slot = jnp.sum(u * hidden[span, :].astype(f32), axis=1, keepdims=True)
            for j, hit in hits(g):
                back[g * group + j] = jnp.sum(jnp.where(hit, slot, 0.0), axis=0, keepdims=True)


def through(every, meta, down, hidden):
    n, tok, cols = every.shape
    slots, width = hidden.shape
    most = slots // n
    group = 1
    while (group * most) % 16:
        group *= 2
    part = 512
    return pl.pallas_call(
        functools.partial(through_kernel, group, most, tok),
        grid=(cols // part,),
        out_shape=(jax.ShapeDtypeStruct((slots, cols), bf16),
                   jax.ShapeDtypeStruct((slots, width), bf16),
                   jax.ShapeDtypeStruct((n, 1, tok), f32)),
        in_specs=[pl.BlockSpec((n, tok, part), lambda i: (0, 0, i)),
                  pl.BlockSpec((n, 2, tok), lambda i: (0, 0, 0)),
                  pl.BlockSpec((width, part), lambda i: (0, i)),
                  pl.BlockSpec((slots, width), lambda i: (0, 0))],
        out_specs=(pl.BlockSpec((slots, part), lambda i: (0, i)),
                   pl.BlockSpec((slots, width), lambda i: (0, 0)),
                   pl.BlockSpec((n, 1, tok), lambda i: (0, 0, 0))),
        scratch_shapes=[pltpu.VMEM((n, group * most, tok), bf16),
                        pltpu.VMEM((slots, 1), f32),
                        pltpu.VMEM((slots, width), f32),
                        pltpu.VMEM((slots, part), bf16)],
        compiler_params=pltpu.CompilerParams(vmem_limit_bytes=56 << 20),
        cost_estimate=pl.CostEstimate(flops=2 * slots * cols * (width + tok), transcendentals=0,
                                      bytes_accessed=2 * (n * tok * cols + 2 * slots * cols)),
        name="through",
    )(every, meta, down, hidden)


def weight_kernel(hidden, scaled, out, turned):
    @pl.when(pl.program_id(0) == 0)
    def _():
        turned[...] = hidden[...].T

    out[...] = jnp.dot(turned[...], scaled[...], preferred_element_type=f32).astype(bf16)


def weight(hidden, scaled):
    slots, width = hidden.shape
    cols = scaled.shape[1]
    part = 512
    return pl.pallas_call(
        weight_kernel,
        grid=(cols // part,),
        out_shape=jax.ShapeDtypeStruct((width, cols), bf16),
        in_specs=[pl.BlockSpec((slots, width), lambda i: (0, 0)),
                  pl.BlockSpec((slots, part), lambda i: (0, i))],
        out_specs=pl.BlockSpec((width, part), lambda i: (0, i)),
        scratch_shapes=[pltpu.VMEM((width, slots), bf16)],
        compiler_params=pltpu.CompilerParams(vmem_limit_bytes=48 << 20),
        cost_estimate=pl.CostEstimate(flops=2 * slots * cols * width, transcendentals=0,
                                      bytes_accessed=2 * (slots * cols + slots * width + cols * width)),
        name="weight",
    )(hidden, scaled)


def gate_kernel(ep_n, node_n, dp_n, back, mask, chosen, whole, tokens, out, home, part, inbox,
                home_send, home_recv, send_a, recv_a, send_b, recv_b):
    ep, node, dp = lax.axis_index("ep"), lax.axis_index("node"), lax.axis_index("dp")
    n = ep_n * node_n
    me = ep * node_n + node
    everyone = n * dp_n

    def at(p, q):
        return {"ep": p // node_n, "node": p % node_n, "dp": q}

    def peer(j):
        return lax.rem(me + j % n, n), lax.rem(dp + j // n, dp_n)

    barrier = pltpu.get_barrier_semaphore()

    def greet(j, carry):
        p, q = peer(j)
        pl.semaphore_signal(barrier, inc=1, device_id=at(p, q), device_id_type=MESH)
        return carry

    lax.fori_loop(1, everyone, greet, 0)
    pl.semaphore_wait(barrier, everyone - 1)

    def home_copy(j):
        p, q = peer(j)
        return pltpu.make_async_remote_copy(
            src_ref=back.at[p], dst_ref=home.at[dp, me],
            send_sem=home_send.at[j], recv_sem=home_recv.at[j],
            device_id=at(p, q), device_id_type=MESH)

    def go_home(j, carry):
        home_copy(j).start()
        return carry

    lax.fori_loop(1, everyone, go_home, 0)
    home[dp, me] = back[me]

    def came_home(j, carry):
        home_copy(j).wait()
        return carry

    lax.fori_loop(1, everyone, came_home, 0)
    route = home[0, :, 0, :]
    for q in range(1, dp_n):
        route = route + home[q, :, 0, :]
    picked = chosen[...]
    all_of = whole[...]
    mixed = jnp.sum(route * picked, axis=0, keepdims=True) / all_of
    score_grad = route_scale / all_of * (route - mixed)
    logit = (mask[...] * score_grad * picked * (1.0 - picked)).astype(bf16)
    lanes = part.shape[2]
    for i in range(part.shape[1]):
        part[:, i, :] = jnp.dot(logit, tokens[:, i * lanes:(i + 1) * lanes], preferred_element_type=f32)

    def to_owner(j):
        p = lax.rem(me + j, n)
        return pltpu.make_async_remote_copy(
            src_ref=part.at[p], dst_ref=inbox.at[j],
            send_sem=send_a.at[j], recv_sem=recv_a.at[j],
            device_id=at(p, dp), device_id_type=MESH)

    def start_a(j, carry):
        to_owner(j).start()
        return carry

    def wait_a(j, carry):
        to_owner(j).wait()
        return carry

    lax.fori_loop(1, n, start_a, 0)
    lax.fori_loop(1, n, wait_a, 0)
    out[me] = lax.fori_loop(1, n, lambda j, acc: acc + inbox[j], part[me])

    def spread(j):
        p = lax.rem(me + j, n)
        return pltpu.make_async_remote_copy(
            src_ref=out.at[me], dst_ref=out.at[me],
            send_sem=send_b.at[j], recv_sem=recv_b.at[j],
            device_id=at(p, dp), device_id_type=MESH)

    def start_b(j, carry):
        spread(j).start()
        return carry

    def wait_b(j, carry):
        spread(j).wait()
        return carry

    lax.fori_loop(1, n, start_b, 0)
    lax.fori_loop(1, n, wait_b, 0)


def gate(ep_n, node_n, dp_n, back, mask, chosen, total, tokens):
    n = ep_n * node_n
    tok, cols = tokens.shape
    lanes = 128
    shape = (n, cols // lanes, lanes)
    dma = pltpu.SemaphoreType.DMA
    return pl.pallas_call(
        functools.partial(gate_kernel, ep_n, node_n, dp_n),
        out_shape=jax.ShapeDtypeStruct(shape, f32),
        in_specs=[VM] * 5,
        out_specs=VM,
        scratch_shapes=[pltpu.VMEM((dp_n, n, 1, tok), f32),
                        pltpu.VMEM(shape, f32), pltpu.VMEM(shape, f32),
                        dma((n * dp_n,)), dma((n * dp_n,)),
                        dma((n,)), dma((n,)), dma((n,)), dma((n,))],
        compiler_params=pltpu.CompilerParams(collective_id=1, has_side_effects=True,
                                             vmem_limit_bytes=24 << 20),
        cost_estimate=pl.CostEstimate(flops=2 * tok * cols * n, transcendentals=0,
                                      bytes_accessed=8 * n * cols),
        name="gate",
    )(back, mask, chosen, total, tokens).reshape(n, cols)


def body(ep_n, node_n, dp_n, grad_out, tokens, scores, expert_ids, hidden_act, down_weight):
    inner = 2 if ep_n <= 8 else 8
    mask, chosen, total, gains, rank = router(scores, expert_ids)
    place = jnp.stack([rank, gains.astype(f32)], axis=1)
    every, meta = gather(ep_n, inner, node_n, grad_out, place)
    hidden = hidden_act[0]
    scaled, partial, back = through(every, meta, down_weight[0], hidden)
    hidden_grad = lax.psum_scatter(partial, "dp", scatter_dimension=0, tiled=True)[None]
    gate_grad = gate(ep_n, node_n, dp_n, back, mask, chosen, total, tokens)
    weight_grad = weight(hidden, scaled)[None]
    return (weight_grad, hidden_grad, gate_grad)


def solution(mesh):
    sizes = [mesh.shape[a] for a in ("ep", "node", "dp")]
    return jax.shard_map(
        functools.partial(body, *sizes),
        mesh=mesh,
        in_specs=(
            P(AX, "dp"),
            P(AX, "dp"),
            P(AX, None),
            P(AX, None),
            P(AX, None, None),
            P(AX, None, "dp"),
        ),
        out_specs=(P(AX, None, "dp"), P(AX, "dp", None), P(None, "dp")),
        check_vma=False,
    )
```

profile of v0, /device:TPU:0, one launch (start us, length us, event | category | flops | bytes accessed | tf_op | source)
XLA Modules:
  0.0 174.2 jit_solution(16086790751873072314)
XLA Ops:
  7.2 0.0 reduce-scatter.2.cloned.1.call-start
  7.2 1.0 slice_bitcast_fusion.7
  8.2 0.1 fusion
  8.3 0.7 fusion.2
  9.1 0.0 copy-start
  9.1 1.2 copy-done
  10.3 91.8 %gather.1 = (bf16[16,128,3584]{2,1,0:T(8,128)(2,1)S(1)}, f32[16,2,128]{2,1,0:T(2,128)S(1)}) custom-call(bf16[128,3584]{1,0:T(8,128)(2,1)S(1)} %copy-done, f32[16,2,128]{2,1,0:T(2,128)S(1)} %copy.10.place), custom_call_target="tpu_custom_call" | custom-call | tf_op jit(solution)/shard_map/gather/pallas_call | solution.py:225
  102.1 0.0 copy-start.3
  102.1 5.2 %copy-done.3 = bf16[16,128,3584]{2,1,0:T(8,128)(2,1)} copy-done((bf16[16,128,3584]{2,1,0:T(8,128)(2,1)}, bf16[16,128,3584]{2,1,0:T(8,128)(2,1)S(1)}, u32[]{:S(2)}) %copy-start.3) | copy-done | bytes 14680088
  107.3 0.0 copy-start.5
  107.3 0.6 copy-done.5
  107.9 0.0 copy-start.1
  107.9 21.1 %through.1 = (bf16[1280,3584]{1,0:T(8,128)(2,1)}, bf16[1280,1024]{1,0:T(8,128)(2,1)}, f32[16,1,128]{2,1,0:T(1,128)}) custom-call(bf16[16,128,3584]{2,1,0:T(8,128)(2,1)} %copy-done.3, f32[16,2,128]{2,1,0:T(2,128)} %copy-done.5, bf16[1024,3584]{1,0:T(8,128)(2,1)} %bitcast.40, bf16[1280,1024]{1,0:T(8,128)(2,1)} %bitcast.36), custom_call_target="tpu_custom_call" | custom-call | flops 10569646080 | bytes 33030144 | tf_op jit(solution)/shard_map/through/pallas_call | solution.py:293
  129.0 0.0 reduce-scatter.2.cloned.1.call-update
  129.0 0.0 copy-done.1
  129.0 0.0 copy-start.2
  129.0 0.7 copy-done.2
  129.7 20.8 %gate.1 = f32[16,28,128]{2,1,0:T(8,128)S(1)} custom-call(f32[16,1,128]{2,1,0:T(1,128)S(1)} %copy-done.2, f32[16,128]{1,0:T(8,128)S(1)} %get-tuple-element.15.mask, f32[16,128]{1,0:T(8,128)S(1)} %get-tuple-element.14.chosen, f32[1,128]{1,0:T(1,128)S(1)} %bitcast.35, bf16[128,3584]{1,0:T(8,128)(2,1)S(1)} %copy-done.1), custom_call_target="tpu_custom_call" | custom-call | flops 14680064 | bytes 458752 | tf_op jit(solution)/shard_map/gate/pallas_call | solution.py:442
  150.5 0.8 copy.13
  151.3 0.0 copy-start.4
  151.3 1.8 %copy-done.4 = bf16[1,1280,1024]{2,1,0:T(8,128)(2,1)S(1)} copy-done((bf16[1,1280,1024]{2,1,0:T(8,128)(2,1)S(1)}, bf16[1,1280,1024]{2,1,0:T(8,128)(2,1)}, u32[]{:S(2)}) %copy-start.4) | copy-done | bytes 2621464
  153.1 14.2 %weight.1 = bf16[1024,3584]{1,0:T(8,128)(2,1)} custom-call(bf16[1280,1024]{1,0:T(8,128)(2,1)S(1)} %bitcast.37, bf16[1280,3584]{1,0:T(8,128)(2,1)} %get-tuple-element.10.scaled), custom_call_target="tpu_custom_call" | custom-call | flops 9395240960 | bytes 19136512 | tf_op jit(solution)/shard_map/weight/pallas_call | solution.py:329
  167.4 0.0 reduce-scatter.2.cloned.1.call-done
  (3 shorter events, 0.0 us)
Async XLA Ops:
  7.2 160.2 %reduce-scatter.2.cloned.1.call-start = ((), (), s32[]{:S(2)}) async-start(), calls=%async_computation.1 | async-start | bytes 3932160 | tf_op jit(solution)/shard_map/reduce_scatter | solution.py:466
  9.1 1.2 copy-start
  102.1 5.2 %copy-start.3 = (bf16[16,128,3584]{2,1,0:T(8,128)(2,1)}, bf16[16,128,3584]{2,1,0:T(8,128)(2,1)S(1)}, u32[]{:S(2)}) copy-start(bf16[16,128,3584]{2,1,0:T(8,128)(2,1)S(1)} %get-tuple-element.8.every) | copy-start | bytes 44040196
  107.3 0.6 copy-start.5
  107.9 21.1 %copy-start.1 = (bf16[128,3584]{1,0:T(8,128)(2,1)S(1)}, bf16[128,3584]{1,0:T(8,128)(2,1)}, u32[]{:S(2)}) copy-start(bf16[128,3584]{1,0:T(8,128)(2,1)} %tokens.1) | copy-start | bytes 2752516
  129.0 0.7 copy-start.2
  151.3 1.8 %copy-start.4 = (bf16[1,1280,1024]{2,1,0:T(8,128)(2,1)S(1)}, bf16[1,1280,1024]{2,1,0:T(8,128)(2,1)}, u32[]{:S(2)}) copy-start(bf16[1,1280,1024]{2,1,0:T(8,128)(2,1)} %param.10) | copy-start | bytes 7864324
Sparse Core Ops, SparseCore 0:
  129.1 37.4 reduce-scatter.1
where the time goes:
time: 175 us; the launch traced here: 174 us
  Pallas kernels  148 us (85%)
  between operations  14.1 us (8%)
  local copies, waits for them, and re-layouts  11.3 us (6%)
    pallas_call x1, Pallas kernels, gather(): pl.pallas_call(functools.partial(gather_kernel, ep_n, inner, node_n), out...  91.8 us
    pallas_call x1, Pallas kernels, through(): pl.pallas_call(functools.partial(through_kernel, group, most, tok), grid=...  21.1 us
    pallas_call x1, Pallas kernels, gate(): pl.pallas_call(functools.partial(gate_kernel, ep_n, node_n, dp_n), out_sh...  20.8 us
    pallas_call x1, Pallas kernels, weight(): pl.pallas_call(weight_kernel, grid=(cols // part,), out_shape=jax.ShapeDt...  14.2 us
    unnamed x13, local copies, waits for them, and re-layouts  10.3 us
  transfers between devices with their start and end apart: 1, of which 0 were waited for; matrix products, arithmetic and copies ran while one was open for 0% of the time, Pallas kernels for 20%

commit v1 on v0

--- a/solution.py
+++ b/solution.py
@@ -36,7 +36,9 @@
 ANY = pl.BlockSpec(memory_space=pl.ANY)
 
 
-def gather_kernel(ep_n, inner, node_n, block, place, every, meta, local_sem,
+def gather_kernel(ep_n, inner, node_n, part, block, place, down_in, hidden_in,
+                  every, scaled_out, partial_out, back,
+                  meta, down, hidden, scaled, partial, held, acc, local_sem, load_sem, held_sem, out_sem,
                   send, recv, meta_send, meta_recv):
     outer = ep_n // inner
     ep, node = lax.axis_index("ep"), lax.axis_index("node")
@@ -50,6 +52,10 @@
     def source(zz, xx, cc):
         return (zz * inner + xx) * node_n + cc
 
+    load_down = pltpu.make_async_copy(down_in, down, load_sem.at[0])
+    load_hidden = pltpu.make_async_copy(hidden_in, hidden, load_sem.at[1])
+    load_down.start()
+    load_hidden.start()
     barrier = pltpu.get_barrier_semaphore()
 
     def greet(j, carry):
@@ -125,40 +131,55 @@
     keep.start()
     meta[me] = place[me]
 
-    def z_rows(t):
-        if t == 0:
-            return [(z >= 0, z, None)]
-        return [(z >= t, z - t, True), (z + t < outer, z + t, False)]
-
-    def x_step(t):
-        for exists, row, _ in z_rows(t):
-            for d in range(1, inner):
-                s_low = source(row, x - d, node)
-                s_high = source(row, x + d, node)
-
-                @when(exists, x >= d)
-                def _():
-                    arrived(s_low)
-                    start_core(s_low)
-
-                    @pl.when(can_xu)
-                    def _():
-                        push(2, s_low, dev(z, x + 1, node))
-
-                @when(exists, x + d < inner)
-                def _():
-                    arrived(s_high)
-                    start_core(s_high)
-
-                    @pl.when(can_xd)
-                    def _():
-                        push(3, s_high, dev(z, x - 1, node))
-
-    for t in range(1, outer):
-        for exists, row, below in z_rows(t):
+    def sides(t):
+        return [(z >= t, z - t, True), (jnp.logical_and(t >= 1, z + t < outer), z + t, False)]
+
+    slots = scaled.shape[1]
+    tok, cols = held.shape
+
+    def work(s):
+        fetch = pltpu.make_async_copy(every.at[s], held, held_sem)
+        fetch.start()
+        spot = meta[s]
+        hit = spot[0:1, :] == lax.broadcasted_iota(jnp.int32, (slots, tok), 0).astype(f32)
+        gain = jnp.sum(jnp.where(hit, spot[1:2, :], 0.0), axis=1, keepdims=True)
+        pick = hit.astype(f32).astype(bf16)
+        acc[...] = jnp.zeros_like(acc)
+        fetch.wait()
+
+        def columns(i, carry):
+            span = pl.ds(pl.multiple_of(i * part, part), part)
+            got = jnp.dot(pick, held[:, span], preferred_element_type=f32)
+            scaled[s, :, span] = (got * gain).astype(bf16)
+            acc[...] += lax.dot_general(got.astype(bf16), down[:, span], (((1,), (1,)), ((), ())),
+                                        preferred_element_type=f32)
+            return carry
+
+        lax.fori_loop(0, cols // part, columns, 0)
+        u = acc[...]
+        partial[s] = (gain * u).astype(bf16)
+        slot = jnp.sum(u * hidden[s].astype(f32), axis=1, keepdims=True)
+        back[s] = jnp.sum(jnp.where(hit, slot, 0.0), axis=0, keepdims=True)
+        pltpu.make_async_copy(scaled.at[s], scaled_out.at[s], out_sem.at[0, s]).start()
+        pltpu.make_async_copy(partial.at[s], partial_out.at[s], out_sem.at[1, s]).start()
+
+    def told(j, carry):
+        pltpu.make_async_remote_copy(
+            src_ref=place.at[0], dst_ref=meta.at[0],
+            send_sem=meta_send.at[j], recv_sem=meta_recv.at[j],
+            device_id=dev(z, x, node), device_id_type=MESH).wait()
+        return carry
+
+    keep.wait()
+    load_down.wait()
+    load_hidden.wait()
+    lax.fori_loop(1, n, told, 0)
+
+    def step(t, carry):
+        for exists, row, below in sides(t):
             s = source(row, x, node)
 
-            @pl.when(exists)
+            @when(exists, t >= 1)
             def _():
                 arrived(s)
                 if below:
@@ -171,17 +192,56 @@
                         push(1, s, dev(z - 1, x, node))
                 start_x(s, can_xu, can_xd)
                 start_core(s)
-        x_step(t - 1)
-    x_step(outer - 1)
-
-    keep.wait()
-
-    def rest(e, carry):
-        for k in range(1, node_n):
-            arrived(e * node_n + lax.rem(node + k, node_n))
-        return carry
-
-    lax.fori_loop(0, ep_n, rest, 0)
+
+        for exists, row, _ in sides(t - 1):
+            for far in range(1, inner):
+                s_low = source(row, x - far, node)
+                s_high = source(row, x + far, node)
+
+                @when(exists, t >= 1, x >= far)
+                def _():
+                    arrived(s_low)
+                    start_core(s_low)
+
+                    @pl.when(can_xu)
+                    def _():
+                        push(2, s_low, dev(z, x + 1, node))
+
+                @when(exists, t >= 1, x + far < inner)
+                def _():
+                    arrived(s_high)
+                    start_core(s_high)
+
+                    @pl.when(can_xd)
+                    def _():
+                        push(3, s_high, dev(z, x - 1, node))
+
+        def each(i, carry):
+            e, c = i % ep_n, lax.rem(node + i // ep_n, node_n)
+            row, col = e // inner, e % inner
+            away = jnp.abs(row - z) + jnp.where(col == x, 0, 1)
+            s = e * node_n + c
+
+            @pl.when(away == t)
+            def _():
+                @pl.when(c != node)
+                def _():
+                    arrived(s)
+
+                work(s)
+            return carry
+
+        lax.fori_loop(0, n, each, 0)
+        return carry
+
+    lax.fori_loop(0, outer + 1, step, 0)
+
+    def stored(s, carry):
+        pltpu.make_async_copy(scaled.at[s], scaled_out.at[s], out_sem.at[0, s]).wait()
+        pltpu.make_async_copy(partial.at[s], partial_out.at[s], out_sem.at[1, s]).wait()
+        return carry
+
+    lax.fori_loop(0, n, stored, 0)
 
     def ended(e, carry):
         s = e * node_n + node
@@ -210,108 +270,34 @@
 
     lax.fori_loop(0, ep_n, ended, 0)
 
-    def told(j, carry):
-        pltpu.make_async_remote_copy(
-            src_ref=place.at[0], dst_ref=meta.at[0],
-            send_sem=meta_send.at[j], recv_sem=meta_recv.at[j],
-            device_id=dev(z, x, node), device_id_type=MESH).wait()
-        return carry
-
-    lax.fori_loop(1, n, told, 0)
-
-
-def gather(ep_n, inner, node_n, grad_out, place):
+
+def gather(ep_n, inner, node_n, grad_out, place, down, hidden):
     n = ep_n * node_n
+    tok, cols = grad_out.shape
+    width = down.shape[0]
+    slots = hidden.shape[1]
+    part = 512 if cols % 512 == 0 else cols
+    dma = pltpu.SemaphoreType.DMA
     return pl.pallas_call(
-        functools.partial(gather_kernel, ep_n, inner, node_n),
-        out_shape=(jax.ShapeDtypeStruct((n,) + grad_out.shape, grad_out.dtype),
-                   jax.ShapeDtypeStruct(place.shape, place.dtype)),
-        in_specs=[ANY, VM],
-        out_specs=(ANY, VM),
+        functools.partial(gather_kernel, ep_n, inner, node_n, part),
+        out_shape=(jax.ShapeDtypeStruct((n, tok, cols), bf16),
+                   jax.ShapeDtypeStruct((n, slots, cols), bf16),
+                   jax.ShapeDtypeStruct((n, slots, width), bf16),
+                   jax.ShapeDtypeStruct((n, 1, tok), f32)),
+        in_specs=[ANY, VM, ANY, ANY],
+        out_specs=(ANY, ANY, ANY, VM),
         scratch_shapes=[
-            pltpu.SemaphoreType.DMA,
-            pltpu.SemaphoreType.DMA((3 + node_n, n)),
-            pltpu.SemaphoreType.DMA((n,)),
-            pltpu.SemaphoreType.DMA((n,)),
-            pltpu.SemaphoreType.DMA((n,)),
+            pltpu.VMEM(place.shape, f32), pltpu.VMEM((width, cols), bf16),
+            pltpu.VMEM((n, slots, width), bf16), pltpu.VMEM((n, slots, cols), bf16),
+            pltpu.VMEM((n, slots, width), bf16), pltpu.VMEM((tok, cols), bf16),
+            pltpu.VMEM((slots, width), f32),
+            dma, dma((2,)), dma, dma((2, n)),
+            dma((3 + node_n, n)), dma((n,)), dma((n,)), dma((n,)),
         ],
         compiler_params=pltpu.CompilerParams(collective_id=0, has_side_effects=True,
-                                             vmem_limit_bytes=16 << 20),
+                                             vmem_limit_bytes=56 << 20),
         name="gather",
-    )(grad_out, place)
-
-
-def through_kernel(group, most, tok, every, meta, down, hidden, scaled, partial, back, pick, gain, total, plain):
-    step, steps = pl.program_id(0), pl.num_programs(0)
-    n = every.shape[0]
-    rows = group * most
-
-    def hits(g):
-        for j in range(group):
-            ranks = meta[g * group + j, 0:1, :]
-            local = lax.broadcasted_iota(jnp.int32, (rows, tok), 0).astype(f32) - float(j * most)
-            yield j, (ranks == local)
-
-    @pl.when(step == 0)
-    def _():
-        total[...] = jnp.zeros_like(total)
-        for g in range(n // group):
-            own = jnp.zeros((rows, 1), f32)
-            for j, hit in hits(g):
-                own = own + jnp.sum(jnp.where(hit, meta[g * group + j, 1:2, :], 0.0), axis=1, keepdims=True)
-                pick[g * group + j] = hit.astype(f32).astype(bf16)
-            gain[g * rows:(g + 1) * rows, :] = own
-
-    for g in range(n // group):
-        got = jnp.zeros((rows, every.shape[2]), f32)
-        for j in range(group):
-            got = got + jnp.dot(pick[g * group + j], every[g * group + j], preferred_element_type=f32)
-        span = slice(g * rows, (g + 1) * rows)
-        scaled[span, :] = (got * gain[span, :]).astype(bf16)
-        plain[span, :] = got.astype(bf16)
-    total[...] += lax.dot_general(plain[...], down[...], (((1,), (1,)), ((), ())), preferred_element_type=f32)
-
-    @pl.when(step == steps - 1)
-    def _():
-        for g in range(n // group):
-            span = slice(g * rows, (g + 1) * rows)
-            u = total[span, :]
-            partial[span, :] = (gain[span, :] * u).astype(bf16)
-            slot = jnp.sum(u * hidden[span, :].astype(f32), axis=1, keepdims=True)
-            for j, hit in hits(g):
-                back[g * group + j] = jnp.sum(jnp.where(hit, slot, 0.0), axis=0, keepdims=True)
-
-
-def through(every, meta, down, hidden):
-    n, tok, cols = every.shape
-    slots, width = hidden.shape
-    most = slots // n
-    group = 1
-    while (group * most) % 16:
-        group *= 2
-    part = 512
-    return pl.pallas_call(
-        functools.partial(through_kernel, group, most, tok),
-        grid=(cols // part,),
-        out_shape=(jax.ShapeDtypeStruct((slots, cols), bf16),
-                   jax.ShapeDtypeStruct((slots, width), bf16),
-                   jax.ShapeDtypeStruct((n, 1, tok), f32)),
-        in_specs=[pl.BlockSpec((n, tok, part), lambda i: (0, 0, i)),
-                  pl.BlockSpec((n, 2, tok), lambda i: (0, 0, 0)),
-                  pl.BlockSpec((width, part), lambda i: (0, i)),
-                  pl.BlockSpec((slots, width), lambda i: (0, 0))],
-        out_specs=(pl.BlockSpec((slots, part), lambda i: (0, i)),
-                   pl.BlockSpec((slots, width), lambda i: (0, 0)),
-                   pl.BlockSpec((n, 1, tok), lambda i: (0, 0, 0))),
-        scratch_shapes=[pltpu.VMEM((n, group * most, tok), bf16),
-                        pltpu.VMEM((slots, 1), f32),
-                        pltpu.VMEM((slots, width), f32),
-                        pltpu.VMEM((slots, part), bf16)],
-        compiler_params=pltpu.CompilerParams(vmem_limit_bytes=56 << 20),
-        cost_estimate=pl.CostEstimate(flops=2 * slots * cols * (width + tok), transcendentals=0,
-                                      bytes_accessed=2 * (n * tok * cols + 2 * slots * cols)),
-        name="through",
-    )(every, meta, down, hidden)
+    )(grad_out, place, down, hidden)
 
 
 def weight_kernel(hidden, scaled, out, turned):
@@ -325,7 +311,7 @@
 def weight(hidden, scaled):
     slots, width = hidden.shape
     cols = scaled.shape[1]
-    part = 512
+    part = 512 if cols % 512 == 0 else cols
     return pl.pallas_call(
         weight_kernel,
         grid=(cols // part,),
@@ -460,9 +446,15 @@
     inner = 2 if ep_n <= 8 else 8
     mask, chosen, total, gains, rank = router(scores, expert_ids)
     place = jnp.stack([rank, gains.astype(f32)], axis=1)
-    every, meta = gather(ep_n, inner, node_n, grad_out, place)
+    n = ep_n * node_n
     hidden = hidden_act[0]
-    scaled, partial, back = through(every, meta, down_weight[0], hidden)
+    slots, width = hidden.shape
+    most = slots // n
+    fill = -most % 16
+    apart = jnp.pad(hidden.reshape(n, most, width), ((0, 0), (0, fill), (0, 0)))
+    every, scaled, partial, back = gather(ep_n, inner, node_n, grad_out, place, down_weight[0], apart)
+    scaled = scaled[:, :most].reshape(slots, -1)
+    partial = partial[:, :most].reshape(slots, width)
     hidden_grad = lax.psum_scatter(partial, "dp", scatter_dimension=0, tiled=True)[None]
     gate_grad = gate(ep_n, node_n, dp_n, back, mask, chosen, total, tokens)
     weight_grad = weight(hidden, scaled)[None]

time: 175 us -> 187 us (1.069)
  Pallas kernels: 148 us -> 167 us
  local copies, waits for them, and re-layouts: 11.3 us -> 3.78 us
    pallas_call x2 -> x1, Pallas kernels: 113 us -> 132 us  [gather(): pl.pallas_call(functools.partial(gather_kernel, ep_n, inner, node_n, part...]
    unnamed x13 -> x11, local copies, waits for them, and re-layouts: 10.3 us -> 2.18 us
  transfers between devices with their start and end apart: 1 -> 1, of which waited for: 0 -> 0; matrix products, arithmetic and copies ran while one was open for 0% -> 0% of each run, Pallas kernels for 20% -> 19%
where the time goes in v1:
time: 187 us; the launch traced here: 186 us
  Pallas kernels  167 us (89%)
  between operations  14.1 us (8%)
  local copies, waits for them, and re-layouts  3.78 us (2%)
    pallas_call x1, Pallas kernels, gather(): pl.pallas_call(functools.partial(gather_kernel, ep_n, inner, node_n, part...  132 us
    pallas_call x1, Pallas kernels, gate(): pl.pallas_call(functools.partial(gate_kernel, ep_n, node_n, dp_n), out_sh...  20.7 us
    pallas_call x1, Pallas kernels, weight(): pl.pallas_call(weight_kernel, grid=(cols // part,), out_shape=jax.ShapeDt...  14.2 us
  transfers between devices with their start and end apart: 1, of which 0 were waited for; matrix products, arithmetic and copies ran while one was open for 0% of the time, Pallas kernels for 19%

profile of v1, /device:TPU:0, one launch (start us, length us, event | category | flops | bytes accessed | tf_op | source)
XLA Modules:
  0.0 185.9 jit_solution(17797140966519423756)
XLA Ops:
  7.2 0.0 copy-start.1
  7.2 0.0 reduce-scatter.2.cloned.1.call-start
  7.2 1.0 slice_bitcast_fusion.7
  8.2 0.1 fusion
  8.3 0.7 fusion.2
  9.1 0.0 copy-start.3
  9.1 0.6 copy.10.place
  9.7 0.0 copy-done.3
  9.7 0.0 copy-start
  9.7 132.2 %gather.1 = (bf16[16,128,3584]{2,1,0:T(8,128)(2,1)}, bf16[16,80,3584]{2,1,0:T(8,128)(2,1)}, bf16[16,80,1024]{2,1,0:T(8,128)(2,1)}, f32[16,1,128]{2,1,0:T(1,128)}) custom-call(bf16[128,3584]{1,0:T(8,128)(2,1)} %block.1, f32[16,2,128]{2,1,0:T(2,128)} %copy.10.place, bf16[1024,3584]{1,0:T(8,128)(2,1)} %bitcast.41, bf16[16,80,1024]{2,1,0:T(8,128)(2,1)} %bitcast.37), custom_call_target="tpu_custom_call" | custom-call | tf_op jit(solution)/shard_map/gather/pallas_call | solution.py:281
  141.9 0.0 reduce-scatter.2.cloned.1.call-update
  141.9 0.0 copy-done.1
  141.9 0.0 copy-start.2
  141.9 0.7 copy-done.2
  142.6 0.0 copy-start.4
  142.6 0.7 copy-done.4
  143.3 20.7 %gate.1 = f32[16,28,128]{2,1,0:T(8,128)S(1)} custom-call(f32[16,1,128]{2,1,0:T(1,128)S(1)} %copy-done.2, f32[16,128]{1,0:T(8,128)S(1)} %get-tuple-element.11.mask, f32[16,128]{1,0:T(8,128)S(1)} %get-tuple-element.10.chosen, f32[1,128]{1,0:T(1,128)S(1)} %bitcast.40, bf16[128,3584]{1,0:T(8,128)(2,1)S(1)} %copy-done.1), custom_call_target="tpu_custom_call" | custom-call | flops 14680064 | bytes 458752 | tf_op jit(solution)/shard_map/gate/pallas_call | solution.py:428
  164.0 0.8 copy.13
  164.8 0.0 copy-done
  164.8 14.2 %weight.1 = bf16[1024,3584]{1,0:T(8,128)(2,1)} custom-call(bf16[1280,1024]{1,0:T(8,128)(2,1)S(1)} %bitcast.38, bf16[1280,3584]{1,0:T(8,128)(2,1)} %bitcast.45), custom_call_target="tpu_custom_call" | custom-call | flops 9395240960 | bytes 19136512 | tf_op jit(solution)/shard_map/weight/pallas_call | solution.py:315
  179.1 0.0 reduce-scatter.2.cloned.1.call-done
  (2 shorter events, 0.0 us)
Async XLA Ops:
  7.2 134.8 %copy-start.1 = (bf16[128,3584]{1,0:T(8,128)(2,1)S(1)}, bf16[128,3584]{1,0:T(8,128)(2,1)}, u32[]{:S(2)}) copy-start(bf16[128,3584]{1,0:T(8,128)(2,1)} %tokens.1) | copy-start | bytes 2752516
  7.2 171.9 %reduce-scatter.2.cloned.1.call-start = ((), (), s32[]{:S(2)}) async-start(), calls=%async_computation.1 | async-start | bytes 3932160 | tf_op jit(solution)/shard_map/reduce_scatter | solution.py:458
  9.1 0.6 copy-start.3
  9.7 155.1 %copy-start = (bf16[1,1280,1024]{2,1,0:T(8,128)(2,1)S(1)}, bf16[1,1280,1024]{2,1,0:T(8,128)(2,1)}, u32[]{:S(2)}) copy-start(bf16[1,1280,1024]{2,1,0:T(8,128)(2,1)} %param.10) | copy-start | bytes 7864324
  141.9 0.7 copy-start.2
  142.6 0.7 copy-start.4
Sparse Core Ops, SparseCore 0:
  142.0 36.9 reduce-scatter.1

commit v2 on v1

--- a/solution.py
+++ b/solution.py
@@ -38,7 +38,7 @@
 
 def gather_kernel(ep_n, inner, node_n, part, block, place, down_in, hidden_in,
                   every, scaled_out, partial_out, back,
-                  meta, down, hidden, scaled, partial, held, acc, local_sem, load_sem, held_sem, out_sem,
+                  meta, down, turned, hidden, scaled, partial, held, acc, local_sem, load_sem, held_sem, out_sem,
                   send, recv, meta_send, meta_recv):
     outer = ep_n // inner
     ep, node = lax.axis_index("ep"), lax.axis_index("node")
@@ -135,33 +135,45 @@
         return [(z >= t, z - t, True), (jnp.logical_and(t >= 1, z + t < outer), z + t, False)]
 
     slots = scaled.shape[1]
-    tok, cols = held.shape
-
-    def work(s):
-        fetch = pltpu.make_async_copy(every.at[s], held, held_sem)
-        fetch.start()
-        spot = meta[s]
-        hit = spot[0:1, :] == lax.broadcasted_iota(jnp.int32, (slots, tok), 0).astype(f32)
-        gain = jnp.sum(jnp.where(hit, spot[1:2, :], 0.0), axis=1, keepdims=True)
-        pick = hit.astype(f32).astype(bf16)
+    tok, cols = held.shape[1:]
+
+    def turn(i, carry):
+        span = pl.ds(pl.multiple_of(i * part, part), part)
+        turned[span, :] = down[:, span].T
+        return carry
+
+    def work(e):
+        own = range(node_n)
+        fetch = [pltpu.make_async_copy(every.at[e * node_n + c], held.at[c], held_sem.at[c]) for c in own]
+        for one in fetch:
+            one.start()
+        spots = [meta[e * node_n + c] for c in own]
+        names = lax.broadcasted_iota(jnp.int32, (slots, tok), 0).astype(f32)
+        hits = [spot[0:1, :] == names for spot in spots]
+        gains = [jnp.sum(jnp.where(hits[c], spots[c][1:2, :], 0.0), axis=1, keepdims=True) for c in own]
+        picks = [hit.astype(f32).astype(bf16) for hit in hits]
         acc[...] = jnp.zeros_like(acc)
-        fetch.wait()
+        for one in fetch:
+            one.wait()
 
         def columns(i, carry):
             span = pl.ds(pl.multiple_of(i * part, part), part)
-            got = jnp.dot(pick, held[:, span], preferred_element_type=f32)
-            scaled[s, :, span] = (got * gain).astype(bf16)
-            acc[...] += lax.dot_general(got.astype(bf16), down[:, span], (((1,), (1,)), ((), ())),
-                                        preferred_element_type=f32)
+            got = [jnp.dot(picks[c], held[c, :, span], preferred_element_type=f32) for c in own]
+            for c in own:
+                scaled[e * node_n + c, :, span] = (got[c] * gains[c]).astype(bf16)
+            acc[...] += jnp.dot(jnp.concatenate(got, axis=0).astype(bf16), turned[span, :],
+                                preferred_element_type=f32)
             return carry
 
         lax.fori_loop(0, cols // part, columns, 0)
-        u = acc[...]
-        partial[s] = (gain * u).astype(bf16)
-        slot = jnp.sum(u * hidden[s].astype(f32), axis=1, keepdims=True)
-        back[s] = jnp.sum(jnp.where(hit, slot, 0.0), axis=0, keepdims=True)
-        pltpu.make_async_copy(scaled.at[s], scaled_out.at[s], out_sem.at[0, s]).start()
-        pltpu.make_async_copy(partial.at[s], partial_out.at[s], out_sem.at[1, s]).start()
+        for c in own:
+            s = e * node_n + c
+            u = acc[c * slots:(c + 1) * slots, :]
+            partial[s] = (gains[c] * u).astype(bf16)
+            slot = jnp.sum(u * hidden[s].astype(f32), axis=1, keepdims=True)
+            back[s] = jnp.sum(jnp.where(hits[c], slot, 0.0), axis=0, keepdims=True)
+            pltpu.make_async_copy(scaled.at[s], scaled_out.at[s], out_sem.at[0, s]).start()
+            pltpu.make_async_copy(partial.at[s], partial_out.at[s], out_sem.at[1, s]).start()
 
     def told(j, carry):
         pltpu.make_async_remote_copy(
@@ -173,6 +185,7 @@
     keep.wait()
     load_down.wait()
     load_hidden.wait()
+    lax.fori_loop(0, cols // part, turn, 0)
     lax.fori_loop(1, n, told, 0)
 
     def step(t, carry):
@@ -216,22 +229,18 @@
                     def _():
                         push(3, s_high, dev(z, x - 1, node))
 
-        def each(i, carry):
-            e, c = i % ep_n, lax.rem(node + i // ep_n, node_n)
+        def each(e, carry):
             row, col = e // inner, e % inner
             away = jnp.abs(row - z) + jnp.where(col == x, 0, 1)
-            s = e * node_n + c
 
             @pl.when(away == t)
             def _():
-                @pl.when(c != node)
-                def _():
-                    arrived(s)
-
-                work(s)
+                for k in range(1, node_n):
+                    arrived(e * node_n + lax.rem(node + k, node_n))
+                work(e)
             return carry
 
-        lax.fori_loop(0, n, each, 0)
+        lax.fori_loop(0, ep_n, each, 0)
         return carry
 
     lax.fori_loop(0, outer + 1, step, 0)
@@ -288,10 +297,11 @@
         out_specs=(ANY, ANY, ANY, VM),
         scratch_shapes=[
             pltpu.VMEM(place.shape, f32), pltpu.VMEM((width, cols), bf16),
+            pltpu.VMEM((cols, width), bf16),
             pltpu.VMEM((n, slots, width), bf16), pltpu.VMEM((n, slots, cols), bf16),
-            pltpu.VMEM((n, slots, width), bf16), pltpu.VMEM((tok, cols), bf16),
-            pltpu.VMEM((slots, width), f32),
-            dma, dma((2,)), dma, dma((2, n)),
+            pltpu.VMEM((n, slots, width), bf16), pltpu.VMEM((node_n, tok, cols), bf16),
+            pltpu.VMEM((node_n * slots, width), f32),
+            dma, dma((2,)), dma((node_n,)), dma((2, n)),
             dma((3 + node_n, n)), dma((n,)), dma((n,)), dma((n,)),
         ],
         compiler_params=pltpu.CompilerParams(collective_id=0, has_side_effects=True,

time: 187 us -> 172 us (0.920)
  Pallas kernels: 167 us -> 152 us
    pallas_call x1, Pallas kernels: 132 us -> 115 us  [gather(): pl.pallas_call(functools.partial(gather_kernel, ep_n, inner, node_n, part...]
    pallas_call x1, Pallas kernels: 20.7 us -> 22.7 us  [gate(): pl.pallas_call(functools.partial(gate_kernel, ep_n, node_n, dp_n), out_sh...]
  transfers between devices with their start and end apart: 1 -> 1, of which waited for: 0 -> 1; matrix products, arithmetic and copies ran while one was open for 0% -> 0% of each run, Pallas kernels for 19% -> 22%
where the time goes in v2:
time: 172 us; the launch traced here: 171 us
  Pallas kernels  152 us (88%)
  between operations  14.1 us (8%)
  local copies, waits for them, and re-layouts  3.78 us (2%)
    pallas_call x1, Pallas kernels, gather(): pl.pallas_call(functools.partial(gather_kernel, ep_n, inner, node_n, part...  115 us
    pallas_call x1, Pallas kernels, gate(): pl.pallas_call(functools.partial(gate_kernel, ep_n, node_n, dp_n), out_sh...  22.7 us
    pallas_call x1, Pallas kernels, weight(): pl.pallas_call(weight_kernel, grid=(cols // part,), out_shape=jax.ShapeDt...  14.3 us
  transfers between devices with their start and end apart: 1, of which 1 were waited for; matrix products, arithmetic and copies ran while one was open for 0% of the time, Pallas kernels for 22%

profile of v2, /device:TPU:0, one launch (start us, length us, event | category | flops | bytes accessed | tf_op | source)
XLA Modules:
  0.0 171.3 jit_solution(14349586188707652655)
XLA Ops:
  7.2 0.0 copy-start.1
  7.2 0.0 reduce-scatter.2.cloned.1.call-start
  7.2 1.0 slice_bitcast_fusion.7
  8.2 0.1 fusion
  8.3 0.7 fusion.2
  9.1 0.0 copy-start.3
  9.1 0.6 copy.10.place
  9.7 0.0 copy-done.3
  9.7 0.0 copy-start
  9.7 115.0 %gather.1 = (bf16[16,128,3584]{2,1,0:T(8,128)(2,1)}, bf16[16,80,3584]{2,1,0:T(8,128)(2,1)}, bf16[16,80,1024]{2,1,0:T(8,128)(2,1)}, f32[16,1,128]{2,1,0:T(1,128)}) custom-call(bf16[128,3584]{1,0:T(8,128)(2,1)} %block.1, f32[16,2,128]{2,1,0:T(2,128)} %copy.10.place, bf16[1024,3584]{1,0:T(8,128)(2,1)} %bitcast.41, bf16[16,80,1024]{2,1,0:T(8,128)(2,1)} %bitcast.37), custom_call_target="tpu_custom_call" | custom-call | tf_op jit(solution)/shard_map/gather/pallas_call | solution.py:290
  124.8 0.0 reduce-scatter.2.cloned.1.call-update
  124.8 0.0 copy-done.1
  124.8 0.0 copy-start.2
  124.8 0.7 copy-done.2
  125.5 0.0 copy-start.4
  125.5 0.7 copy-done.4
  126.2 22.7 %gate.1 = f32[16,28,128]{2,1,0:T(8,128)S(1)} custom-call(f32[16,1,128]{2,1,0:T(1,128)S(1)} %copy-done.2, f32[16,128]{1,0:T(8,128)S(1)} %get-tuple-element.11.mask, f32[16,128]{1,0:T(8,128)S(1)} %get-tuple-element.10.chosen, f32[1,128]{1,0:T(1,128)S(1)} %bitcast.40, bf16[128,3584]{1,0:T(8,128)(2,1)S(1)} %copy-done.1), custom_call_target="tpu_custom_call" | custom-call | flops 14680064 | bytes 458752 | tf_op jit(solution)/shard_map/gate/pallas_call | solution.py:438
  148.8 0.8 copy.13
  149.7 0.0 copy-done
  149.7 14.3 %weight.1 = bf16[1024,3584]{1,0:T(8,128)(2,1)} custom-call(bf16[1280,1024]{1,0:T(8,128)(2,1)S(1)} %bitcast.38, bf16[1280,3584]{1,0:T(8,128)(2,1)} %bitcast.45), custom_call_target="tpu_custom_call" | custom-call | flops 9395240960 | bytes 19136512 | tf_op jit(solution)/shard_map/weight/pallas_call | solution.py:325
  164.0 0.5 reduce-scatter.2.cloned.1.call-done
  (2 shorter events, 0.0 us)
Async XLA Ops:
  7.2 117.6 %copy-start.1 = (bf16[128,3584]{1,0:T(8,128)(2,1)S(1)}, bf16[128,3584]{1,0:T(8,128)(2,1)}, u32[]{:S(2)}) copy-start(bf16[128,3584]{1,0:T(8,128)(2,1)} %tokens.1) | copy-start | bytes 2752516
  7.2 157.3 %reduce-scatter.2.cloned.1.call-start = ((), (), s32[]{:S(2)}) async-start(), calls=%async_computation.1 | async-start | bytes 3932160 | tf_op jit(solution)/shard_map/reduce_scatter | solution.py:468
  9.1 0.6 copy-start.3
  9.7 139.9 %copy-start = (bf16[1,1280,1024]{2,1,0:T(8,128)(2,1)S(1)}, bf16[1,1280,1024]{2,1,0:T(8,128)(2,1)}, u32[]{:S(2)}) copy-start(bf16[1,1280,1024]{2,1,0:T(8,128)(2,1)} %param.10) | copy-start | bytes 7864324
  124.8 0.7 copy-start.2
  125.5 0.7 copy-start.4
Sparse Core Ops, SparseCore 0:
  124.9 39.5 reduce-scatter.1

commit v3 on v2

--- a/solution.py
+++ b/solution.py
@@ -285,7 +285,7 @@
     tok, cols = grad_out.shape
     width = down.shape[0]
     slots = hidden.shape[1]
-    part = 512 if cols % 512 == 0 else cols
+    part = 1792 if cols % 1792 == 0 else cols
     dma = pltpu.SemaphoreType.DMA
     return pl.pallas_call(
         functools.partial(gather_kernel, ep_n, inner, node_n, part),

time: 172 us -> 169 us (0.983)
  Pallas kernels: 152 us -> 149 us
    pallas_call x1, Pallas kernels: 115 us -> 112 us  [gather(): pl.pallas_call(functools.partial(gather_kernel, ep_n, inner, node_n, part...]
where the time goes in v3:
time: 169 us; the launch traced here: 168 us
  Pallas kernels  149 us (88%)
  between operations  14.1 us (8%)
  local copies, waits for them, and re-layouts  3.78 us (2%)
    pallas_call x1, Pallas kernels, gather(): pl.pallas_call(functools.partial(gather_kernel, ep_n, inner, node_n, part...  112 us
    pallas_call x1, Pallas kernels, gate(): pl.pallas_call(functools.partial(gate_kernel, ep_n, node_n, dp_n), out_sh...  22.7 us
    pallas_call x1, Pallas kernels, weight(): pl.pallas_call(weight_kernel, grid=(cols // part,), out_shape=jax.ShapeDt...  14.3 us
  transfers between devices with their start and end apart: 1, of which 1 were waited for; matrix products, arithmetic and copies ran while one was open for 0% of the time, Pallas kernels for 22%

profile of v3, /device:TPU:0, one launch (start us, length us, event | category | flops | bytes accessed | tf_op | source)
XLA Modules:
  0.0 168.5 jit_solution(11448697060471735774)
XLA Ops:
  7.2 0.0 copy-start.1
  7.2 0.0 reduce-scatter.2.cloned.1.call-start
  7.2 1.0 slice_bitcast_fusion.7
  8.2 0.1 fusion
  8.3 0.7 fusion.2
  9.1 0.0 copy-start.3
  9.1 0.6 copy.10.place
  9.7 0.0 copy-done.3
  9.7 0.0 copy-start
  9.7 112.2 %gather.1 = (bf16[16,128,3584]{2,1,0:T(8,128)(2,1)}, bf16[16,80,3584]{2,1,0:T(8,128)(2,1)}, bf16[16,80,1024]{2,1,0:T(8,128)(2,1)}, f32[16,1,128]{2,1,0:T(1,128)}) custom-call(bf16[128,3584]{1,0:T(8,128)(2,1)} %block.1, f32[16,2,128]{2,1,0:T(2,128)} %copy.10.place, bf16[1024,3584]{1,0:T(8,128)(2,1)} %bitcast.41, bf16[16,80,1024]{2,1,0:T(8,128)(2,1)} %bitcast.37), custom_call_target="tpu_custom_call" | custom-call | tf_op jit(solution)/shard_map/gather/pallas_call | solution.py:290
  121.9 0.0 reduce-scatter.2.cloned.1.call-update
  122.0 0.0 copy-done.1
  122.0 0.0 copy-start.2
  122.0 0.7 copy-done.2
  122.7 0.0 copy-start.4
  122.7 0.7 copy-done.4
  123.3 22.7 %gate.1 = f32[16,28,128]{2,1,0:T(8,128)S(1)} custom-call(f32[16,1,128]{2,1,0:T(1,128)S(1)} %copy-done.2, f32[16,128]{1,0:T(8,128)S(1)} %get-tuple-element.11.mask, f32[16,128]{1,0:T(8,128)S(1)} %get-tuple-element.10.chosen, f32[1,128]{1,0:T(1,128)S(1)} %bitcast.40, bf16[128,3584]{1,0:T(8,128)(2,1)S(1)} %copy-done.1), custom_call_target="tpu_custom_call" | custom-call | flops 14680064 | bytes 458752 | tf_op jit(solution)/shard_map/gate/pallas_call | solution.py:438
  146.1 0.8 copy.13
  146.9 0.0 copy-done
  146.9 14.3 %weight.1 = bf16[1024,3584]{1,0:T(8,128)(2,1)} custom-call(bf16[1280,1024]{1,0:T(8,128)(2,1)S(1)} %bitcast.38, bf16[1280,3584]{1,0:T(8,128)(2,1)} %bitcast.45), custom_call_target="tpu_custom_call" | custom-call | flops 9395240960 | bytes 19136512 | tf_op jit(solution)/shard_map/weight/pallas_call | solution.py:325
  161.2 0.4 reduce-scatter.2.cloned.1.call-done
  (2 shorter events, 0.0 us)
Async XLA Ops:
  7.2 114.8 %copy-start.1 = (bf16[128,3584]{1,0:T(8,128)(2,1)S(1)}, bf16[128,3584]{1,0:T(8,128)(2,1)}, u32[]{:S(2)}) copy-start(bf16[128,3584]{1,0:T(8,128)(2,1)} %tokens.1) | copy-start | bytes 2752516
  7.2 154.5 %reduce-scatter.2.cloned.1.call-start = ((), (), s32[]{:S(2)}) async-start(), calls=%async_computation.1 | async-start | bytes 3932160 | tf_op jit(solution)/shard_map/reduce_scatter | solution.py:468
  9.1 0.6 copy-start.3
  9.7 137.2 %copy-start = (bf16[1,1280,1024]{2,1,0:T(8,128)(2,1)S(1)}, bf16[1,1280,1024]{2,1,0:T(8,128)(2,1)}, u32[]{:S(2)}) copy-start(bf16[1,1280,1024]{2,1,0:T(8,128)(2,1)} %param.10) | copy-start | bytes 7864324
  122.0 0.7 copy-start.2
  122.7 0.7 copy-start.4
Sparse Core Ops, SparseCore 0:
  122.1 39.5 reduce-scatter.1
